TPU v7x, 1024 devices: a whole 8x8x8 slice. The times are simulated.
1024 devices in a mesh: group: 8 (over z), member: 128 (over y, x, core).
Axes of the slice: x: 8, y: 8, z: 8, core: 2. Of those that a mesh axis runs over, the one named last changes fastest.
Arguments:
- tokens: bfloat16 [1024, 3584], P(('group', 'member')), may hold values from -6 to 6
- grad_out: bfloat16 [1024, 3584], P(('group', 'member')), may hold values from -6 to 6
- route_token: int32 [8, 8, 8, 16], P('group'), may hold values from 0 to 127, as said below
- route_count: int32 [8, 8, 8], P('group'), may hold values from 0 to 16, as said below
- route_prob: float32 [8, 8, 8, 16], P('group'), may hold values from 0.05 to 0.6
- w_gate: bfloat16 [1024, 64, 3584], P(('group', 'member')), may hold values from -0.09375 to 0.09375
- w_up: bfloat16 [1024, 64, 3584], P(('group', 'member')), may hold values from -0.09375 to 0.09375
- w_down: bfloat16 [1024, 64, 3584], P(('group', 'member')), may hold values from -0.1875 to 0.1875
Outputs:
- grad_tokens: bfloat16 [1024, 3584], P(('group', 'member'))
- grad_gate: bfloat16 [1024, 64, 3584], P(('group', 'member'))
- grad_up: bfloat16 [1024, 64, 3584], P(('group', 'member'))
- grad_down: bfloat16 [1024, 64, 3584], P(('group', 'member'))
Inputs may be any that keep to these rules, and one draw needn't show every extreme that they name: Each token of a source group is routed to 2 different experts in each of 4 different groups. An expert keeps, for each source group, the first 16 of the tokens routed to it in token order and drops the rest; route_token lists the kept tokens in that order, all different, and slots at or past route_count hold 0. In every draw one expert keeps 16 tokens from every source group. `route_count`: the number of kept tokens of each source group for each expert; 16 is reached in every draw.
All inputs are finite; a program needn't handle non-finite values.
Results may differ from a plain program's by a relative error of at most 0.0058.
Values may be sent and summed in bfloat16 or wider, within the bound.
A program may use at most 32 MiB of HBM per device.

v0:
```python
import jax
import jax.numpy as jnp
from jax import lax
from jax.sharding import PartitionSpec as P


def slice_backward(rows_x, rows_scaled, gate_weight, up_weight, down_weight):
    gate_value = jnp.dot(rows_x, gate_weight.T, preferred_element_type=jnp.float32)
    up_value = jnp.dot(rows_x, up_weight.T, preferred_element_type=jnp.float32)
    sigma_gate = jax.nn.sigmoid(gate_value)
    active = gate_value * sigma_gate
    hidden = (active * up_value).astype(jnp.bfloat16)
    d_hidden = jnp.dot(rows_scaled, down_weight.T, preferred_element_type=jnp.float32)
    d_gate = (d_hidden * up_value * sigma_gate * (1.0 + gate_value * (1.0 - sigma_gate))).astype(
        jnp.bfloat16
    )
    d_up = (d_hidden * active).astype(jnp.bfloat16)
    grad_down = jnp.dot(hidden.T, rows_scaled, preferred_element_type=jnp.float32).astype(
        jnp.bfloat16
    )
    grad_gate = jnp.dot(d_gate.T, rows_x, preferred_element_type=jnp.float32).astype(jnp.bfloat16)
    grad_up = jnp.dot(d_up.T, rows_x, preferred_element_type=jnp.float32).astype(jnp.bfloat16)
    partial_rows = jnp.dot(d_gate, gate_weight, preferred_element_type=jnp.float32)
    partial_rows = partial_rows + jnp.dot(d_up, up_weight, preferred_element_type=jnp.float32)
    return (grad_gate, grad_up, grad_down, partial_rows)


def shards(tokens, grad_out, route_token, route_count, route_prob, w_gate, w_up, w_down):
    groups = route_token.shape[1]
    capacity = route_token.shape[3]
    features = tokens.shape[1]
    block_rows = groups * capacity
    split_count = max(8, lax.axis_size("member") // 8)
    expert_local = lax.axis_index("member") // split_count
    slot_tokens = lax.dynamic_index_in_dim(route_token[0], expert_local, 1, keepdims=False)
    slot_counts = lax.dynamic_index_in_dim(route_count[0], expert_local, 1, keepdims=False)
    slot_probs = lax.dynamic_index_in_dim(route_prob[0], expert_local, 1, keepdims=False)
    slot_index = jnp.arange(capacity, dtype=jnp.int32)[None, :]
    live = (slot_index < slot_counts[:, None]).astype(jnp.float32)
    slot_weights = (slot_probs * live).reshape(-1)
    flat_slots = slot_tokens.reshape(-1)
    group_x, group_dy = (
        lax.all_gather(tokens, "member", axis=0, tiled=True),
        lax.all_gather(grad_out, "member", axis=0, tiled=True),
    )
    picked_x = jnp.take(group_x, flat_slots, axis=0)
    picked_dy = jnp.take(group_dy, flat_slots, axis=0)
    scaled = (slot_weights[:, None] * picked_dy.astype(jnp.float32)).astype(jnp.bfloat16)
    send_x = picked_x.reshape(groups, capacity, features)
    send_scaled = scaled.reshape(groups, capacity, features)
    rows_x, rows_scaled = (
        lax.all_to_all(send_x, "group", split_axis=0, concat_axis=0, tiled=True),
        lax.all_to_all(send_scaled, "group", split_axis=0, concat_axis=0, tiled=True),
    )
    grad_gate, grad_up, grad_down, partial_rows = slice_backward(
        rows_x.reshape(block_rows, features),
        rows_scaled.reshape(block_rows, features),
        w_gate[0],
        w_up[0],
        w_down[0],
    )
    returned = lax.all_to_all(
        partial_rows.reshape(groups, capacity, features),
        "group",
        split_axis=0,
        concat_axis=0,
        tiled=True,
    )
    returned = returned.reshape(block_rows, features)
    row_numbers = jnp.arange(tokens.shape[0] * lax.axis_size("member"), dtype=jnp.int32)
    selector = (row_numbers[:, None] == flat_slots[None, :]).astype(jnp.float32)
    summed = lax.psum_scatter(
        jnp.dot(
            selector, returned, precision=lax.Precision.HIGHEST, preferred_element_type=jnp.float32
        ),
        "member",
        scatter_dimension=0,
        tiled=True,
    )
    return (summed.astype(jnp.bfloat16), grad_gate[None], grad_up[None], grad_down[None])


def solution(mesh):
    placed = (
        P(("group", "member"), None),
        P(("group", "member"), None),
        P("group", None, None, None),
        P("group", None, None),
        P("group", None, None, None),
        P(("group", "member"), None, None),
        P(("group", "member"), None, None),
        P(("group", "member"), None, None),
    )
    return jax.shard_map(
        shards,
        mesh=mesh,
        in_specs=placed,
        out_specs=(
            P(("group", "member"), None),
            P(("group", "member"), None, None),
            P(("group", "member"), None, None),
            P(("group", "member"), None, None),
        ),
        check_vma=False,
    )
```

profile of v0, /device:TPU:1, one launch (start us, length us, event | category | flops | bytes accessed | tf_op | source)
XLA Modules:
  0.0 721.7 jit_solution(14213864732144753587)
XLA Ops:
  0.7 0.8 dynamic-slice_reduce_fusion.2
  1.6 62.5 %all-gather.1 = bf16[128,1,3584]{2,1,0:T(2,128)(2,1)S(1)} all-gather(bf16[1,1,3584]{2,1,0:T(2,128)(2,1)} %bitcast.57), channel_id=1, replica_groups=mesh['group'=8,'member'=128] {'member'}, dimensions={0}, use_global_device_ids=true | all-gather | bytes 924672 | tf_op jit(solution)/shard_map/all_gather | solution.py:43
  64.2 1.1 gather_fusion.1
  65.4 1.1 broadcast_select_fusion
  66.4 8.3 %all-to-all-start.1 = ((bf16[8,16,3584]{2,1,0:T(8,128)(2,1)}), bf16[8,16,3584]{2,1,0:T(8,128)(2,1)S(1)}, u32[]{:S(2)}, u32[]{:S(2)}) async-start(bf16[8,16,3584]{2,1,0:T(8,128)(2,1)} %bitcast.5), calls=%async_computation.1 | async-start | bytes 1835008 | tf_op jit(solution)/shard_map/all_to_all | solution.py:52
  75.2 0.8 dynamic-slice_reduce_fusion
  76.0 49.8 %all-gather = bf16[128,1,3584]{2,1,0:T(2,128)(2,1)S(1)} all-gather(bf16[1,1,3584]{2,1,0:T(2,128)(2,1)S(1)} %bitcast.58), channel_id=1, replica_groups=mesh['group'=8,'member'=128] {'member'}, dimensions={0}, use_global_device_ids=true | all-gather | bytes 924672 | tf_op jit(solution)/shard_map/all_gather | solution.py:44
  126.0 1.1 gather_fusion
  127.1 1.3 multiply_convert_fusion
  128.4 7.0 all-to-all-start
  135.9 0.4 fusion.8
  136.3 25.5 %all-to-all-done = bf16[8,16,3584]{2,1,0:T(8,128)(2,1)S(1)} async-done(((bf16[8,16,3584]{2,1,0:T(8,128)(2,1)}), bf16[8,16,3584]{2,1,0:T(8,128)(2,1)S(1)}, u32[]{:S(2)}, u32[]{:S(2)}) %all-to-all-start) | async-done | bytes 917536 | tf_op jit(solution)/shard_map/all_to_all | solution.py:53
  161.8 0.4 multiply_convert_fusion.2
  162.3 0.4 fusion.3
  162.7 1.6 convolution_add_fusion
  164.3 4.3 all-to-all-start.2
  168.6 1.4 dynamic-slice.3
  170.0 1.0 fusion.1
  171.0 1.0 fusion
  172.1 1.0 fusion.2
  173.1 38.7 %all-to-all-done.2 = f32[8,16,3584]{2,1,0:T(8,128)} async-done(((f32[8,16,3584]{2,1,0:T(8,128)}), f32[8,16,3584]{2,1,0:T(8,128)}, u32[]{:S(2)}, u32[]{:S(2)}) %all-to-all-start.2) | async-done | bytes 1835040 | tf_op jit(solution)/shard_map/all_to_all | solution.py:62
  211.8 2.5 fusion.12
  214.3 506.0 %all-reduce.2 = bf16[128,3584]{1,0:T(8,128)(2,1)S(1)} all-reduce(f32[128,3584]{1,0:T(8,128)S(1)} %fusion.12), channel_id=2, replica_groups=mesh['group'=8,'member'=128] {'member'}, use_global_device_ids=true, to_apply=%region_0.2.clone | all-reduce | flops 458752 | bytes 2752512
  720.4 1.3 dynamic-slice_convert_fusion
  (23 shorter events, 1.2 us)
Async XLA Ops:
  0.6 134.8 %copy-start = (bf16[1,64,3584]{2,1,0:T(8,128)(2,1)S(1)}, bf16[1,64,3584]{2,1,0:T(8,128)(2,1)}, u32[]{:S(2)}) copy-start(bf16[1,64,3584]{2,1,0:T(8,128)(2,1)} %param.15) | copy-start | bytes 1376260
  65.3 9.5 %copy-start.4 = (s32[1,8,8]{2,1,0:T(8,128)S(1)}, s32[1,8,8]{2,1,0:T(8,128)}, u32[]{:S(2)}) copy-start(s32[1,8,8]{2,1,0:T(8,128)} %param.13) | copy-start | bytes 772
  65.4 10.7 %copy-start.3 = (bf16[1,3584]{1,0:T(2,128)(2,1)S(1)}, bf16[1,3584]{1,0:T(2,128)(2,1)}, u32[]{:S(2)}) copy-start(bf16[1,3584]{1,0:T(2,128)(2,1)} %param.11) | copy-start | bytes 21508
  66.4 61.9 %all-to-all-start.1 = ((bf16[8,16,3584]{2,1,0:T(8,128)(2,1)}), bf16[8,16,3584]{2,1,0:T(8,128)(2,1)S(1)}, u32[]{:S(2)}, u32[]{:S(2)}) async-start(bf16[8,16,3584]{2,1,0:T(8,128)(2,1)} %bitcast.5), calls=%async_computation.1 | async-start | bytes 1835008 | tf_op jit(solution)/shard_map/all_to_all | solution.py:52
  128.4 7.5 %copy-start.1 = (bf16[1,64,3584]{2,1,0:T(8,128)(2,1)S(1)}, bf16[1,64,3584]{2,1,0:T(8,128)(2,1)}, u32[]{:S(2)}) copy-start(bf16[1,64,3584]{2,1,0:T(8,128)(2,1)} %param.16) | copy-start | bytes 1376260
  128.4 33.4 %all-to-all-start = ((bf16[8,16,3584]{2,1,0:T(8,128)(2,1)}), bf16[8,16,3584]{2,1,0:T(8,128)(2,1)S(1)}, u32[]{:S(2)}, u32[]{:S(2)}) async-start(bf16[8,16,3584]{2,1,0:T(8,128)(2,1)} %bitcast.56), calls=%async_computation | async-start | bytes 1835008 | tf_op jit(solution)/shard_map/all_to_all | solution.py:53
  135.4 26.4 %copy-start.2 = (bf16[1,64,3584]{2,1,0:T(8,128)(2,1)S(1)}, bf16[1,64,3584]{2,1,0:T(8,128)(2,1)}, u32[]{:S(2)}) copy-start(bf16[1,64,3584]{2,1,0:T(8,128)(2,1)} %param.17) | copy-start | bytes 1376260
  164.3 47.5 %all-to-all-start.2 = ((f32[8,16,3584]{2,1,0:T(8,128)}), f32[8,16,3584]{2,1,0:T(8,128)}, u32[]{:S(2)}, u32[]{:S(2)}) async-start(f32[8,16,3584]{2,1,0:T(8,128)} %bitcast.55), calls=%async_computation.2 | async-start | bytes 3670016 | tf_op jit(solution)/shard_map/all_to_all | solution.py:62
where the time goes:
time: 725 us; the launch traced here: 722 us
  blocking collectives  618 us (85%)
  waiting for transfers between devices  64.2 us (9%)
  starting transfers between devices  19.7 us (3%)
  matrix products  8.98 us (1%)
    unnamed x1, blocking collectives  506 us
    all_gather x1, blocking collectives, shards(): lax.all_gather(tokens, 'member', axis=0, tiled=True)  62.5 us
    all_gather x1, blocking collectives, shards(): lax.all_gather(grad_out, 'member', axis=0, tiled=True)  49.8 us
    all_to_all x1, waiting for transfers between devices, shards(): lax.all_to_all(partial_rows.reshape(groups, capacity, features), 'group',...  38.7 us
    all_to_all x1, waiting for transfers between devices, shards(): lax.all_to_all(send_scaled, 'group', split_axis=0, concat_axis=0, tiled=T...  25.5 us
  transfers between devices with their start and end apart: 3, of which 2 were waited for; matrix products, arithmetic and copies ran while one was open for 1% of the time, Pallas kernels for 0%

commit v1 on v0

v1 whole, which is shorter than its diff:
```python
import functools

import jax
import jax.numpy as jnp
from jax import lax
from jax.experimental import pallas as pl
from jax.experimental.pallas import tpu as pltpu
from jax.sharding import PartitionSpec as P

MESH = pl.DeviceIdType.MESH
CW = 256
F32 = jnp.float32
BF16 = jnp.bfloat16


def dot_nn(a, b):
    return jnp.dot(a, b, preferred_element_type=F32)


def dot_nt(a, b):
    return lax.dot_general(a, b, (((1,), (1,)), ((), ())), preferred_element_type=F32)


def kernel(
    dims,
    x_ref, dy_ref, tok_ref, cnt_ref, prob_ref, wg, wu, wd,
    gt_ref, gg, gu, gd,
    send_a, recv_a, t_all, z_send, rows, w_gu, w_dd, w_sib, acc_gu, acc_dh,
    sel_t, d_pair, d_t, h_t, p_buf, snd, rcv, r2_send, r2_recv, r3_send, r3_recv,
    r4_send, r4_recv, grads,
    w_sem, out_sem, small_send, small_recv, ring_send, ring_recv, sib_send, sib_recv,
    red_send, red_recv,
):
    ng, ny, nx, hs, cap = dims
    nk = 2 * nx
    nc = nk - 2
    nd = nc // 2
    ns = ng * cap
    tg = ny * nk
    half = ns // 2
    far = nx // 2

    z = lax.axis_index("group")
    m = lax.axis_index("member")
    y = m // nk
    k = m % nk
    x = k // 2
    c = k % 2
    sibling = (z, y * nk + 2 * x + (1 - c))
    neighbour = (
        (z, y * nk + 2 * ((x + 1) % nx) + c),
        (z, y * nk + 2 * ((x + nx - 1) % nx) + c),
    )
    reach = ((far, nx - 1 - far), (nx - 1 - far, far))
    routes = k < nc

    def remote(src, dst, send_sem, recv_sem, device):
        return pltpu.make_async_remote_copy(
            src_ref=src, dst_ref=dst, send_sem=send_sem, recv_sem=recv_sem,
            device_id=device, device_id_type=MESH,
        )

    def arrived(ref, sem):
        pltpu.make_async_copy(ref, ref, sem).wait()

    def signal(device):
        pl.semaphore_signal(
            pltpu.get_barrier_semaphore(), inc=1, device_id=device, device_id_type=MESH
        )

    A, B, C, W, X, R2, R3, R4 = range(8)

    loads = [
        pltpu.make_async_copy(wg.at[0], w_gu.at[pl.ds(0, hs)], w_sem.at[0]),
        pltpu.make_async_copy(wu.at[0], w_gu.at[pl.ds(hs, hs)], w_sem.at[1]),
        pltpu.make_async_copy(wd.at[0], w_dd.at[pl.ds(0, hs)], w_sem.at[2]),
        pltpu.make_async_copy(wd.at[0], w_dd.at[pl.ds(hs, hs)], w_sem.at[3]),
    ]
    for load in loads:
        load.start()

    for o in range(1, nk):
        signal((z, y * nk + (k + o) % nk))
    for o in range(1, ny):
        signal((z, ((y + o) % ny) * nk + k))
    for o in range(1, ng):
        signal(((z + o) % ng, m))

    for u in range(2 * nc):
        cols = slice(u * 128, (u + 1) * 128)
        send_a[u // 2, pl.ds(u % 2, 1), :] = x_ref[:, cols].astype(F32)
        send_a[u // 2, pl.ds(2 + u % 2, 1), :] = dy_ref[:, cols].astype(F32)

    pl.semaphore_wait(pltpu.get_barrier_semaphore(), (nk - 1) + (ny - 1) + (ng - 1))

    for o in range(1, nk):
        kk = (k + o) % nk

        @pl.when(kk < nc)
        def _():
            remote(
                send_a.at[kk], recv_a.at[k], small_send.at[A], small_recv.at[A],
                (z, y * nk + kk),
            ).start()

    row = lax.broadcasted_iota(jnp.int32, (ns, cap), 0)
    lane = lax.broadcasted_iota(jnp.int32, (ns, cap), 1)

    def spread(ref):
        wide = jnp.concatenate(
            [
                jnp.broadcast_to(ref[0, i, pl.ds(y, 1), :].astype(F32), (cap, cap))
                for i in range(ng)
            ],
            axis=0,
        )
        return jnp.sum(jnp.where(lane == row % cap, wide, 0.0), axis=1, keepdims=True)

    counts = jnp.concatenate(
        [
            jnp.broadcast_to(cnt_ref[0, pl.ds(i, 1), :].astype(F32), (cap, ny))
            for i in range(ng)
        ],
        axis=0,
    )
    expert = lax.broadcasted_iota(jnp.int32, (ns, ny), 1)
    counts = jnp.sum(jnp.where(expert == y, counts, 0.0), axis=1, keepdims=True)
    slot_token = spread(tok_ref)
    position = (lax.broadcasted_iota(jnp.int32, (ns, 1), 0) % cap).astype(F32)
    live = jnp.where(position < counts, 1.0, 0.0)
    weight = spread(prob_ref) * live
    token = lax.broadcasted_iota(jnp.int32, (ns, tg), 1).astype(F32)
    sel = jnp.where(token == slot_token, 1.0, 0.0)
    sel_t[...] = (sel * live).T.astype(BF16)
    sel = sel.astype(BF16)

    for load in loads:
        load.wait()
    to_sibling = [
        remote(
            w_gu.at[:, pl.ds(pl.multiple_of((2 * i + 1 - c) * CW, CW), CW)], w_sib.at[i],
            small_send.at[W], small_recv.at[W], sibling,
        )
        for i in range(nd)
    ]
    for copy in to_sibling:
        copy.start()

    acc_gu[...] = jnp.zeros_like(acc_gu)
    acc_dh[...] = jnp.zeros_like(acc_dh)

    def block(source, core, h):
        return rows.at[2 * source + core, pl.ds(h * half, half), :]

    @pl.when(routes)
    def _():
        recv_a[k] = send_a[k]
        arrived(recv_a.at[pl.ds(0, nk - 1)], small_recv.at[A])
        t_all[y] = jnp.concatenate([recv_a[:, u, :] for u in range(4)], axis=1).astype(BF16)
        for o in range(1, ny):
            remote(
                t_all.at[y], t_all.at[y], small_send.at[B], small_recv.at[B],
                (z, ((y + o) % ny) * nk + k),
            ).start()
        arrived(t_all.at[pl.ds(0, ny - 1)], small_recv.at[B])
        picked = dot_nn(sel, t_all[...].reshape(tg, 2 * CW))
        z_send[:, :, 0:CW] = picked[:, 0:CW].astype(BF16).reshape(ng, cap, CW)
        z_send[:, :, CW:] = (picked[:, CW:] * weight).astype(BF16).reshape(ng, cap, CW)
        here = pl.ds(pl.multiple_of(z * cap, cap), cap)
        for o in range(1, ng):
            g = (z + o) % ng
            remote(
                z_send.at[g], rows.at[k, here, :], small_send.at[C], small_recv.at[C], (g, m)
            ).start()
        rows[k, here, :] = z_send[z]
        arrived(rows.at[k, pl.ds(0, ns - cap), :], small_recv.at[C])
        for h in range(2):
            for way in range(2):
                if reach[h][way] >= 1:
                    remote(
                        block(x, c, h), block(x, c, h), ring_send.at[way, 0, h],
                        ring_recv.at[way, 1, h], neighbour[way],
                    ).start()
        for h in range(2):
            remote(
                block(x, c, h), block(x, c, h), sib_send.at[0, 0, h], sib_recv.at[0, 0, h],
                sibling,
            ).start()

    def accumulate(source, core):
        chunk = 2 * source + core
        cols = pl.ds(pl.multiple_of(chunk * CW, CW), CW)
        acc_gu[...] += dot_nt(rows[chunk, :, 0:CW], w_gu[:, cols])
        acc_dh[...] += dot_nt(rows[chunk, :, CW:], w_dd[:, cols])

    def source_of(way, t):
        return (x + nx - t) % nx if way == 0 else (x + t) % nx

    def from_sibling(way, t):
        source = source_of(way, t)

        @pl.when(source < nd)
        def _():
            for h in range(2):
                via = way if t < far else (0 if reach[h][0] == far else 1)
                arrived(block(source, 1 - c, h), sib_recv.at[via, t, h])
            accumulate(source, 1 - c)

    @pl.when(routes)
    def _():
        accumulate(x, c)

    for t in range(1, far + 1):
        for h in range(2):
            for way in range(2):
                if t > reach[h][way]:
                    continue
                source = source_of(way, t)

                @pl.when(source < nd)
                def _():
                    arrived(block(source, c, h), ring_recv.at[way, t, h])
                    if t < reach[h][way]:
                        remote(
                            block(source, c, h), block(source, c, h),
                            ring_send.at[way, t, h], ring_recv.at[way, t + 1, h],
                            neighbour[way],
                        ).start()
                    remote(
                        block(source, c, h), block(source, c, h), sib_send.at[way, t, h],
                        sib_recv.at[way, t, h], sibling,
                    ).start()

        for way in range(2 if t < far else 1):
            source = source_of(way, t)

            @pl.when(source < nd)
            def _():
                accumulate(source, c)

        for way in range(2 if t > 1 else 1):
            from_sibling(way, t - 1)
    from_sibling(0, far)

    both = acc_gu[...]
    turned = pltpu.roll(both, hs, 1)
    left = lax.broadcasted_iota(jnp.int32, (ns, 2 * hs), 1) < hs
    gate = jnp.where(left, both, turned)
    up = jnp.where(left, turned, both)
    sg = jax.nn.sigmoid(gate)
    active = gate * sg
    d_hidden = acc_dh[...]
    d_both = jnp.where(
        left, d_hidden * up * sg * (1.0 + gate * (1.0 - sg)), d_hidden * active
    )
    d_pair[c] = d_both.astype(BF16)
    exchange = remote(d_pair.at[c], d_pair.at[c], small_send.at[X], small_recv.at[X], sibling)
    exchange.start()
    d_t[...] = d_both.T.astype(BF16)
    h_t[...] = (active * up).T[0:hs, :].astype(BF16)

    def gradients(chunk):
        cols = slice(chunk * CW, (chunk + 1) * CW)
        grads[0 : 2 * hs, cols] = dot_nn(d_t[...], rows[chunk, :, 0:CW]).astype(BF16)
        grads[2 * hs :, cols] = dot_nn(h_t[...], rows[chunk, :, CW:]).astype(BF16)

    def partial(dest, h):
        lines = slice(h * half, (h + 1) * half)
        cols = pl.ds(pl.multiple_of((2 * dest + c) * CW, CW), CW)
        return dot_nn(d_pair[c, lines, :], w_gu[:, cols]) + dot_nn(
            d_pair[1 - c, lines, :], w_sib[dest]
        )

    def dest_of(way, d):
        return (x + d) % nx if way == 0 else (x + nx - d) % nx

    arrived(w_sib, small_recv.at[W])
    arrived(d_pair.at[0], small_recv.at[X])

    todo = list(range(nc))
    share = -(-nc // far)
    for t in range(1, far + 1):
        moves = [
            (h, way, reach[h][way] + 1 - t)
            for h in range(2)
            for way in range(2)
            if reach[h][way] + 1 - t >= 1
        ]
        if t > 1:
            for h, way, d in moves:
                dest = dest_of(way, d)

                @pl.when(dest < nd)
                def _():
                    p_buf[h, way] = partial(dest, h)

            for chunk in todo[:share]:
                gradients(chunk)
            todo = todo[share:]
        for h, way, d in moves:
            dest = dest_of(way, d)

            @pl.when(dest < nd)
            def _():
                if d == reach[h][way]:
                    value = partial(dest, h)
                else:
                    arrived(rcv.at[way, d, h], red_recv.at[way, d, h])
                    value = p_buf[h, way] + rcv[way, d, h].astype(F32)
                snd[way, d, h] = value.astype(BF16)
                remote(
                    snd.at[way, d, h], rcv.at[way, d - 1, h], red_send.at[way, d, h],
                    red_recv.at[way, d - 1, h], neighbour[way],
                ).start()

    @pl.when(routes)
    def _():
        for h in range(2):
            p_buf[h, 0] = partial(x, h)

    for chunk in todo:
        gradients(chunk)
    stores = [
        pltpu.make_async_copy(grads.at[pl.ds(0, hs)], gg.at[0], out_sem.at[0]),
        pltpu.make_async_copy(grads.at[pl.ds(hs, hs)], gu.at[0], out_sem.at[1]),
        pltpu.make_async_copy(grads.at[pl.ds(2 * hs, hs)], gd.at[0], out_sem.at[2]),
    ]
    for store in stores:
        store.start()

    @pl.when(routes)
    def _():
        for h in range(2):
            value = p_buf[h, 0]
            for way in range(2):
                if reach[h][way] >= 1:
                    arrived(rcv.at[way, 0, h], red_recv.at[way, 0, h])
                    value = value + rcv[way, 0, h].astype(F32)
            span = ng // 2
            r2_send[pl.ds(h * span, span)] = value.astype(BF16).reshape(span, cap, CW)
            for o in range(span):
                s = h * span + (z + o) % span

                @pl.when(s != z)
                def _():
                    remote(
                        r2_send.at[s], r2_recv.at[z], small_send.at[R2], small_recv.at[R2],
                        (s, m),
                    ).start()

        r2_recv[z] = r2_send[z]
        arrived(r2_recv.at[pl.ds(0, ng - 1)], small_recv.at[R2])
        summed = dot_nn(sel_t[...], r2_recv[...].reshape(ns, CW))
        r3_send[...] = summed.astype(BF16).reshape(ny, nk, CW)
        for o in range(1, ny):
            to = (y + o) % ny
            remote(
                r3_send.at[to], r3_recv.at[y], small_send.at[R3], small_recv.at[R3],
                (z, to * nk + k),
            ).start()
        r3_recv[y] = r3_send[y]
        arrived(r3_recv.at[pl.ds(0, ny - 1)], small_recv.at[R3])
        total = jnp.sum(r3_recv[...].astype(F32), axis=0)
        r4_send[:, 0, :] = total[:, 0:128]
        r4_send[:, 1, :] = total[:, 128:]
        for o in range(1, nk):
            to = (k + o) % nk
            remote(
                r4_send.at[to], r4_recv.at[k], small_send.at[R4], small_recv.at[R4],
                (z, y * nk + to),
            ).start()
        r4_recv[k] = r4_send[k]

    exchange.wait_send()
    for way in range(2):
        for h in range(2):
            for t in range(1, reach[h][way]):

                @pl.when(source_of(way, t) < nd)
                def _():
                    arrived(block(0, 0, h), ring_send.at[way, t, h])

            for t in range(1, reach[h][way] + 1):

                @pl.when(source_of(way, t) < nd)
                def _():
                    arrived(block(0, 0, h), sib_send.at[way, t, h])

                @pl.when(dest_of(way, t) < nd)
                def _():
                    arrived(snd.at[way, t, h], red_send.at[way, t, h])

    arrived(w_sib, small_send.at[W])

    @pl.when(routes)
    def _():
        for h in range(2):
            for way in range(2):
                if reach[h][way] >= 1:
                    arrived(block(0, 0, h), ring_send.at[way, 0, h])
            arrived(block(0, 0, h), sib_send.at[0, 0, h])
        arrived(recv_a.at[pl.ds(0, nc - 1)], small_send.at[A])
        arrived(t_all.at[pl.ds(0, ny - 1)], small_send.at[B])
        arrived(z_send.at[pl.ds(0, ng - 1)], small_send.at[C])
        arrived(r2_send.at[pl.ds(0, ng - 1)], small_send.at[R2])
        arrived(r3_send.at[pl.ds(0, ny - 1)], small_send.at[R3])
        arrived(r4_send.at[pl.ds(0, nk - 1)], small_send.at[R4])
        arrived(r4_recv.at[pl.ds(0, nc - 1)], small_recv.at[R4])

    @pl.when(jnp.logical_not(routes))
    def _():
        arrived(recv_a.at[pl.ds(0, nc)], small_send.at[A])
        arrived(r4_recv.at[pl.ds(0, nc)], small_recv.at[R4])

    gt_ref[...] = r4_recv[...]
    for store in stores:
        store.wait()


def shards(mesh, tokens, grad_out, route_token, route_count, route_prob, w_gate, w_up, w_down):
    ng = mesh.shape["group"]
    ny = route_token.shape[2]
    cap = route_token.shape[3]
    nk = mesh.shape["member"] // ny
    nx = nk // 2
    hs, features = w_gate.shape[1:]
    nc = features // CW
    assert nc == nk - 2 and nc * CW == features
    ns, tg, nd, half, far = ng * cap, ny * nk, nc // 2, ng * cap // 2, nx // 2
    vmem = pl.BlockSpec(memory_space=pltpu.VMEM)
    hbm = pl.BlockSpec(memory_space=pl.ANY)
    dma = pltpu.SemaphoreType.DMA
    grad_shape = jax.ShapeDtypeStruct((1, hs, features), BF16)
    grad_rows, grad_gate, grad_up, grad_down = pl.pallas_call(
        functools.partial(kernel, (ng, ny, nx, hs, cap)),
        out_shape=(
            jax.ShapeDtypeStruct((nc, 2, 128), F32),
            grad_shape,
            grad_shape,
            grad_shape,
        ),
        in_specs=[vmem] * 5 + [hbm] * 3,
        out_specs=(vmem, hbm, hbm, hbm),
        scratch_shapes=[
            pltpu.VMEM((nc, 4, 128), F32),
            pltpu.VMEM((nk, 4, 128), F32),
            pltpu.VMEM((ny, nk, 2 * CW), BF16),
            pltpu.VMEM((ng, cap, 2 * CW), BF16),
            pltpu.VMEM((nc, ns, 2 * CW), BF16),
            pltpu.VMEM((2 * hs, features), BF16),
            pltpu.VMEM((2 * hs, features), BF16),
            pltpu.VMEM((nd, 2 * hs, CW), BF16),
            pltpu.VMEM((ns, 2 * hs), F32),
            pltpu.VMEM((ns, 2 * hs), F32),
            pltpu.VMEM((tg, ns), BF16),
            pltpu.VMEM((2, ns, 2 * hs), BF16),
            pltpu.VMEM((2 * hs, ns), BF16),
            pltpu.VMEM((hs, ns), BF16),
            pltpu.VMEM((2, 2, half, CW), F32),
            pltpu.VMEM((2, far + 1, 2, half, CW), BF16),
            pltpu.VMEM((2, far, 2, half, CW), BF16),
            pltpu.VMEM((ng, cap, CW), BF16),
            pltpu.VMEM((ng, cap, CW), BF16),
            pltpu.VMEM((ny, nk, CW), BF16),
            pltpu.VMEM((ny, nk, CW), BF16),
            pltpu.VMEM((nk, 2, 128), F32),
            pltpu.VMEM((nc, 2, 128), F32),
            pltpu.VMEM((3 * hs, features), BF16),
            dma((4,)),
            dma((3,)),
            dma((8,)),
            dma((8,)),
            dma((2, far + 1, 2)),
            dma((2, far + 1, 2)),
            dma((2, far + 1, 2)),
            dma((2, far + 1, 2)),
            dma((2, far + 1, 2)),
            dma((2, far + 1, 2)),
        ],
        compiler_params=pltpu.CompilerParams(
            collective_id=0, has_side_effects=True, vmem_limit_bytes=32 * 1024 * 1024
        ),
        name="routed_backward",
    )(tokens, grad_out, route_token, route_count, route_prob, w_gate, w_up, w_down)
    return grad_rows.reshape(1, features).astype(BF16), grad_gate, grad_up, grad_down


def solution(mesh):
    both = ("group", "member")
    return jax.shard_map(
        functools.partial(shards, mesh),
        mesh=mesh,
        in_specs=(
            P(both, None),
            P(both, None),
            P("group", None, None, None),
            P("group", None, None),
            P("group", None, None, None),
            P(both, None, None),
            P(both, None, None),
            P(both, None, None),
        ),
        out_specs=(
            P(both, None),
            P(both, None, None),
            P(both, None, None),
            P(both, None, None),
        ),
        check_vma=False,
    )
```

time: 725 us -> 97.7 us (0.13)
  blocking collectives: 618 us -> 0 us
  Pallas kernels: 0 us -> 86.9 us
  waiting for transfers between devices: 64.2 us -> 0 us
  starting transfers between devices: 19.7 us -> 0 us
  matrix products: 8.98 us -> 0 us
    unnamed x1 -> x0, blocking collectives: 506 us -> none
    all_gather x2 -> x0, blocking collectives: 112 us -> none  [the longest x1 62.5 us: shards(): lax.all_gather(tokens, 'member', axis=0, tiled=True)]
    pallas_call x0 -> x1, Pallas kernels: none -> 86.9 us  [shards(): pl.pallas_call(functools.partial(kernel, (ng, ny, nx, hs, cap)), out_shap...]
    all_to_all x3 -> x0, waiting for transfers between devices: 64.2 us -> none  [the longest x1 38.7 us: shards(): lax.all_to_all(partial_rows.reshape(groups, capacity, features), 'group',...]
    all_to_all x3 -> x0, starting transfers between devices: 19.7 us -> none  [the longest x1 8.35 us: shards(): lax.all_to_all(send_x, 'group', split_axis=0, concat_axis=0, tiled=True)]
    dot_general x9 -> x0, matrix products: 8.98 us -> none  [the longest x1 2.53 us: shards(): jnp.dot(selector, returned, precision=lax.Precision.HIGHEST, preferred_el...]
    unnamed x13 -> x19, local copies, waits for them, and re-layouts: 1.63 us -> 8.97 us
  transfers between devices with their start and end apart: 3 -> 0, of which waited for: 2 -> 0; matrix products, arithmetic and copies ran while one was open for 1% -> 0% of each run, Pallas kernels for 0% -> 0%
where the time goes in v1:
time: 97.7 us; the launch traced here: 97.2 us
  Pallas kernels  86.9 us (89%)
  local copies, waits for them, and re-layouts  9.59 us (10%)
    pallas_call x1, Pallas kernels, shards(): pl.pallas_call(functools.partial(kernel, (ng, ny, nx, hs, cap)), out_shap...  86.9 us
    unnamed x19, local copies, waits for them, and re-layouts  8.97 us

profile of v1, /device:TPU:1, one launch (start us, length us, event | category | flops | bytes accessed | tf_op | source)
XLA Modules:
  0.0 97.2 jit_solution(9639458653205173171)
XLA Ops:
  0.6 0.0 copy-start
  0.6 1.0 %copy-done = bf16[1,64,3584]{2,1,0:T(8,128)(2,1)S(1)} copy-done((bf16[1,64,3584]{2,1,0:T(8,128)(2,1)S(1)}, bf16[1,64,3584]{2,1,0:T(8,128)(2,1)}, u32[]{:S(2)}) %copy-start) | copy-done | bytes 458776
  1.7 0.0 copy-start.1
  1.7 1.0 %copy-done.1 = bf16[1,64,3584]{2,1,0:T(8,128)(2,1)S(1)} copy-done((bf16[1,64,3584]{2,1,0:T(8,128)(2,1)S(1)}, bf16[1,64,3584]{2,1,0:T(8,128)(2,1)}, u32[]{:S(2)}) %copy-start.1) | copy-done | bytes 458776
  2.7 0.0 copy-start.2
  2.7 1.0 %copy-done.2 = bf16[1,64,3584]{2,1,0:T(8,128)(2,1)S(1)} copy-done((bf16[1,64,3584]{2,1,0:T(8,128)(2,1)S(1)}, bf16[1,64,3584]{2,1,0:T(8,128)(2,1)}, u32[]{:S(2)}) %copy-start.2) | copy-done | bytes 458776
  3.7 0.0 copy-start.3
  3.7 0.8 copy-done.3
  4.4 0.0 copy-start.4
  4.5 0.8 copy-done.4
  5.2 0.0 copy-start.5
  5.2 0.7 copy-done.5
  5.9 0.0 copy-start.6
  5.9 0.7 copy-done.6
  6.6 0.0 copy-start.7
  6.6 0.7 copy-done.7
  7.3 86.9 %routed_backward.1 = (f32[14,2,128]{2,1,0:T(2,128)S(1)}, bf16[1,64,3584]{2,1,0:T(8,128)(2,1)S(1)}, bf16[1,64,3584]{2,1,0:T(8,128)(2,1)S(1)}, bf16[1,64,3584]{2,1,0:T(8,128)(2,1)S(1)}) custom-call(bf16[1,3584]{1,0:T(2,128)(2,1)S(1)} %copy-done.5, bf16[1,3584]{1,0:T(2,128)(2,1)S(1)} %copy-done.6, s32[1,8,8,16]{3,2,1,0:T(8,128)S(1)} %copy-done.3, ...), custom_call_target="tpu_custom_call" | custom-call | tf_op jit(solution)/shard_map/routed_backward/pallas_call | solution.py:434
  94.3 0.6 convert_element_type.15
  94.9 0.8 copy.15
  95.7 0.8 copy.16
  96.4 0.8 copy.17
  (1 shorter events, 0.0 us)
Async XLA Ops:
  0.6 1.0 %copy-start = (bf16[1,64,3584]{2,1,0:T(8,128)(2,1)S(1)}, bf16[1,64,3584]{2,1,0:T(8,128)(2,1)}, u32[]{:S(2)}) copy-start(bf16[1,64,3584]{2,1,0:T(8,128)(2,1)} %wg.1) | copy-start | bytes 1376260
  1.7 1.0 %copy-start.1 = (bf16[1,64,3584]{2,1,0:T(8,128)(2,1)S(1)}, bf16[1,64,3584]{2,1,0:T(8,128)(2,1)}, u32[]{:S(2)}) copy-start(bf16[1,64,3584]{2,1,0:T(8,128)(2,1)} %wu.1) | copy-start | bytes 1376260
  2.7 1.0 %copy-start.2 = (bf16[1,64,3584]{2,1,0:T(8,128)(2,1)S(1)}, bf16[1,64,3584]{2,1,0:T(8,128)(2,1)}, u32[]{:S(2)}) copy-start(bf16[1,64,3584]{2,1,0:T(8,128)(2,1)} %wd.1) | copy-start | bytes 1376260
  3.7 0.8 copy-start.3
  4.4 0.8 copy-start.4
  5.2 0.7 copy-start.5
  5.9 0.7 copy-start.6
  6.6 0.7 copy-start.7

commit v2 on v0

v2 whole, which is shorter than its diff:
```python
import functools

import jax
import jax.numpy as jnp
from jax import lax
from jax.experimental import pallas as pl
from jax.experimental.pallas import tpu as pltpu
from jax.sharding import PartitionSpec as P

MESH = pl.DeviceIdType.MESH
CLASSES = 4
LANES = 128
F32 = jnp.float32
BF16 = jnp.bfloat16


def dot_nn(a, b):
    return jnp.dot(a, b, preferred_element_type=F32)


def dot_nt(a, b):
    return lax.dot_general(a, b, (((1,), (1,)), ((), ())), preferred_element_type=F32)


def kernel(
    dims,
    x_hbm, dy_hbm, tok_hbm, cnt_hbm, prob_hbm, wg, wu, wd,
    gt_ref, gg, gu, gd,
    x_ref, dy_ref, tok_ref, cnt_ref, prob_ref,
    send_a, recv_a, t_all, z_send, rows, w_gu, w_dd, w_sib, acc_gu, acc_dh,
    d_pair, d_t, h_t, p_buf, snd, rcv, r2_send, r2_recv, r3_send, r3_recv,
    r4_send, r4_recv,
    in_sem, w_sem, small_send, small_recv, ring_send, ring_recv, sib_send, sib_recv,
    red_send, red_recv,
):
    ng, ny, nx, hs, cap, cw = dims
    nk = 2 * nx
    ns = ng * cap
    tg = ny * nk
    half = ns // 2
    span = ng // 2
    units = cw // LANES
    pieces = [slice(o, min(o + 256, cw)) for o in range(0, cw, 256)]

    z = lax.axis_index("group")
    m = lax.axis_index("member")
    y = m // nk
    k = m % nk
    x = k // 2
    c = k % 2
    brings = x % CLASSES
    own = k % CLASSES
    other = (own + 2) % CLASSES
    sibling = (z, y * nk + 2 * x + (1 - c))

    def along(steps):
        return (z, y * nk + 2 * ((x + steps + nx) % nx) + c)

    neighbour = (along(1), along(-1))

    def remote(src, dst, send_sem, recv_sem, device):
        return pltpu.make_async_remote_copy(
            src_ref=src, dst_ref=dst, send_sem=send_sem, recv_sem=recv_sem,
            device_id=device, device_id_type=MESH,
        )

    def arrived(ref, sem):
        pltpu.make_async_copy(ref, ref, sem).wait()

    def signal(device):
        pl.semaphore_signal(
            pltpu.get_barrier_semaphore(), inc=1, device_id=device, device_id_type=MESH
        )

    A, B, C, W, X, R2, R3, R4 = range(8)

    for o in range(1, nk):
        signal((z, y * nk + (k + o) % nk))
    for o in range(1, ny):
        signal((z, ((y + o) % ny) * nk + k))
    for o in range(1, ng):
        signal(((z + o) % ng, m))

    inputs = [
        pltpu.make_async_copy(src, dst, in_sem.at[i])
        for i, (src, dst) in enumerate(
            (
                (x_hbm, x_ref), (dy_hbm, dy_ref), (tok_hbm, tok_ref), (cnt_hbm, cnt_ref),
                (prob_hbm, prob_ref),
            )
        )
    ]
    for copy in inputs:
        copy.start()
    loads = [
        pltpu.make_async_copy(wg.at[0], w_gu.at[pl.ds(0, hs)], w_sem.at[0]),
        pltpu.make_async_copy(wu.at[0], w_gu.at[pl.ds(hs, hs)], w_sem.at[1]),
        pltpu.make_async_copy(wd.at[0], w_dd.at[pl.ds(0, hs)], w_sem.at[2]),
        pltpu.make_async_copy(wd.at[0], w_dd.at[pl.ds(hs, hs)], w_sem.at[3]),
    ]
    for load in loads:
        load.start()
    for copy in inputs:
        copy.wait()

    send_a[...] = jnp.zeros_like(send_a)
    for u in range(CLASSES * units):
        cols = slice(u * LANES, (u + 1) * LANES)
        send_a[u // units, pl.ds(u % units, 1), :] = x_ref[:, cols].astype(F32)
        send_a[CLASSES + u // units, pl.ds(u % units, 1), :] = dy_ref[:, cols].astype(F32)

    pl.semaphore_wait(pltpu.get_barrier_semaphore(), (nk - 1) + (ny - 1) + (ng - 1))

    for o in range(1, nk):
        kk = (k + o) % nk
        remote(
            send_a.at[(kk % 2) * CLASSES + kk // 2 % CLASSES], recv_a.at[k], small_send.at[A], small_recv.at[A],
            (z, y * nk + kk),
        ).start()
    recv_a[k] = send_a[c * CLASSES + brings]

    row = lax.broadcasted_iota(jnp.int32, (ns, cap), 0)
    lane = lax.broadcasted_iota(jnp.int32, (ns, cap), 1)

    def spread(ref):
        wide = jnp.concatenate(
            [
                jnp.broadcast_to(ref[0, i, pl.ds(y, 1), :].astype(F32), (cap, cap))
                for i in range(ng)
            ],
            axis=0,
        )
        return jnp.sum(jnp.where(lane == row % cap, wide, 0.0), axis=1, keepdims=True)

    counts = jnp.concatenate(
        [
            jnp.broadcast_to(cnt_ref[0, pl.ds(i, 1), :].astype(F32), (cap, ny))
            for i in range(ng)
        ],
        axis=0,
    )
    expert = lax.broadcasted_iota(jnp.int32, (ns, ny), 1)
    counts = jnp.sum(jnp.where(expert == y, counts, 0.0), axis=1, keepdims=True)
    slot_token = spread(tok_ref)
    position = (lax.broadcasted_iota(jnp.int32, (ns, 1), 0) % cap).astype(F32)
    live = jnp.where(position < counts, 1.0, 0.0)
    core = c.astype(F32)
    factor = spread(prob_ref) * live * core + (1.0 - core)
    token = lax.broadcasted_iota(jnp.int32, (ns, tg), 1).astype(F32)
    sel = jnp.where(token == slot_token, 1.0, 0.0)
    sel_t = (sel * live).T.astype(BF16)
    sel = sel.astype(BF16)

    for load in loads:
        load.wait()
    for i in range(2):
        cols = pl.ds(pl.multiple_of((2 * i + 1 - c) * cw, LANES), cw)
        remote(
            w_gu.at[:, cols], w_sib.at[i], small_send.at[W], small_recv.at[W], sibling
        ).start()

    acc_gu[...] = jnp.zeros_like(acc_gu)
    acc_dh[...] = jnp.zeros_like(acc_dh)

    arrived(recv_a.at[pl.ds(0, nk - 1)], small_recv.at[A])
    t_all[y] = jnp.concatenate([recv_a[:, u, :] for u in range(units)], axis=1).astype(BF16)
    for o in range(1, ny):
        remote(
            t_all.at[y], t_all.at[y], small_send.at[B], small_recv.at[B],
            (z, ((y + o) % ny) * nk + k),
        ).start()
    arrived(t_all.at[pl.ds(0, ny - 1)], small_recv.at[B])
    for piece in pieces:
        width = piece.stop - piece.start
        picked = dot_nn(sel, t_all[:, :, piece].reshape(tg, width)) * factor
        z_send[:, :, piece] = picked.astype(BF16).reshape(ng, cap, width)
    here = pl.ds(pl.multiple_of(z * cap, cap), cap)
    for o in range(1, ng):
        g = (z + o) % ng
        remote(
            z_send.at[g], rows.at[c, brings, here, :], small_send.at[C], small_recv.at[C],
            (g, m),
        ).start()
    rows[c, brings, here, :] = z_send[z]
    arrived(rows.at[c, brings, pl.ds(0, ns - cap), :], small_recv.at[C])

    whole, first, second = pl.ds(0, ns), pl.ds(0, half), pl.ds(half, half)
    moves = ((1, whole), (-1, whole), (2, first), (-2, second))
    for i, (steps, part) in enumerate(moves):
        block = rows.at[c, brings, part, :]
        remote(block, block, ring_send.at[i], ring_recv.at[i], along(steps)).start()

    def share(quarter, part, i):
        block = rows.at[c, quarter, part, :]
        return remote(block, block, sib_send.at[i], sib_recv.at[i], sibling)

    def accumulate(quarter):
        cols = pl.ds(pl.multiple_of(quarter * cw, LANES), cw)
        acc_gu[...] += dot_nt(rows[0, quarter], w_gu[:, cols])
        acc_dh[...] += dot_nt(rows[1, quarter], w_dd[:, cols])

    def source(steps):
        return (brings + CLASSES - steps) % CLASSES

    share(brings, whole, 4).start()
    arrived(rows.at[1 - c, brings], sib_recv.at[4])
    accumulate(brings)
    for stage in (0, 2):
        for i in (stage, stage + 1):
            steps, part = moves[i]
            arrived(rows.at[c, source(steps), part, :], ring_recv.at[i])
            share(source(steps), part, i).start()
        for i in (stage, stage + 1):
            steps, part = moves[i]
            arrived(rows.at[1 - c, source(steps), part, :], sib_recv.at[i])
            if i != 2:
                accumulate(source(steps))

    both = acc_gu[...]
    turned = pltpu.roll(both, hs, 1)
    left = lax.broadcasted_iota(jnp.int32, (ns, 2 * hs), 1) < hs
    gate = jnp.where(left, both, turned)
    up = jnp.where(left, turned, both)
    sg = jax.nn.sigmoid(gate)
    active = gate * sg
    d_hidden = acc_dh[...]
    d_both = jnp.where(
        left, d_hidden * up * sg * (1.0 + gate * (1.0 - sg)), d_hidden * active
    )
    d_pair[c] = d_both.astype(BF16)
    exchange = remote(d_pair.at[c], d_pair.at[c], small_send.at[X], small_recv.at[X], sibling)
    exchange.start()
    d_t[...] = d_both.T.astype(BF16)
    h_t[...] = (active * up).T[0:hs, :].astype(BF16)

    def gradients(quarter):
        for piece in pieces:
            cols = slice(quarter * cw + piece.start, quarter * cw + piece.stop)
            pair = dot_nn(d_t[...], rows[0, quarter, :, piece]).astype(BF16)
            gg[0, :, cols] = pair[0:hs]
            gu[0, :, cols] = pair[hs:]
            gd[0, :, cols] = dot_nn(h_t[...], rows[1, quarter, :, piece]).astype(BF16)

    def partial(quarter, h, piece):
        lines = slice(h * half, (h + 1) * half)
        width = piece.stop - piece.start
        cols = pl.ds(pl.multiple_of(quarter * cw + piece.start, LANES), width)
        return dot_nn(d_pair[c, lines, :], w_gu[:, cols]) + dot_nn(
            d_pair[1 - c, lines, :], w_sib[quarter // 2, :, piece]
        )

    arrived(w_sib, small_recv.at[W])
    arrived(d_pair.at[0], small_recv.at[X])

    for h in range(2):
        for piece in pieces:
            snd[h, :, piece] = partial(other, h, piece).astype(BF16)
        remote(snd.at[h], rcv.at[h], red_send.at[h], red_recv.at[h], neighbour[h]).start()
    for h in range(2):
        for piece in pieces:
            p_buf[h, :, piece] = partial(own, h, piece)
    gradients(0)
    gradients(1)

    for h in range(2):
        arrived(rcv.at[h], red_recv.at[h])
        value = p_buf[h] + rcv[h].astype(F32)
        r2_send[pl.ds(h * span, span)] = value.astype(BF16).reshape(span, cap, cw)
        for o in range(span):
            s = h * span + (z + o) % span

            @pl.when(s != z)
            def _():
                remote(
                    r2_send.at[s], r2_recv.at[z], small_send.at[R2], small_recv.at[R2], (s, m)
                ).start()

    r2_recv[z] = r2_send[z]
    gradients(2)
    gradients(3)
    arrived(r2_recv.at[pl.ds(0, ng - 1)], small_recv.at[R2])
    for piece in pieces:
        width = piece.stop - piece.start
        summed = dot_nn(sel_t, r2_recv[:, :, piece].reshape(ns, width))
        r3_send[:, :, piece] = summed.astype(BF16).reshape(ny, nk, width)
    for o in range(1, ny):
        to = (y + o) % ny
        remote(
            r3_send.at[to], r3_recv.at[y], small_send.at[R3], small_recv.at[R3],
            (z, to * nk + k),
        ).start()
    r3_recv[y] = r3_send[y]
    r4_send[...] = jnp.zeros_like(r4_send)

    arrived(recv_a.at[pl.ds(0, nk - 1)], small_send.at[A])
    arrived(t_all.at[pl.ds(0, ny - 1)], small_send.at[B])
    arrived(z_send.at[pl.ds(0, ng - 1)], small_send.at[C])
    arrived(w_sib, small_send.at[W])
    for i, (steps, part) in enumerate(moves):
        arrived(rows.at[0, 0, part, :], ring_send.at[i])
        arrived(rows.at[0, 0, part, :], sib_send.at[i])
    arrived(rows.at[0, 0], sib_send.at[4])
    for h in range(2):
        arrived(snd.at[h], red_send.at[h])
    exchange.wait_send()
    arrived(r2_send.at[pl.ds(0, ng - 1)], small_send.at[R2])

    arrived(r3_recv.at[pl.ds(0, ny - 1)], small_recv.at[R3])
    for u in range(units):
        cols = slice(u * LANES, (u + 1) * LANES)
        r4_send[:, u, :] = jnp.sum(r3_recv[:, :, cols].astype(F32), axis=0)
    for o in range(1, nk):
        to = (k + o) % nk
        remote(
            r4_send.at[to], r4_recv.at[k], small_send.at[R4], small_recv.at[R4],
            (z, y * nk + to),
        ).start()
    r4_recv[k] = r4_send[k]
    arrived(r3_send.at[pl.ds(0, ny - 1)], small_send.at[R3])
    arrived(r4_recv.at[pl.ds(0, nk - 1)], small_recv.at[R4])
    for quarter in range(CLASSES):
        total = r4_recv[quarter]
        for k2 in range(quarter + CLASSES, nk, CLASSES):
            total = total + r4_recv[k2]
        for u in range(units):
            cols = slice((quarter * units + u) * LANES, (quarter * units + u + 1) * LANES)
            gt_ref[:, cols] = total[u : u + 1, :].astype(BF16)
    arrived(r4_send.at[pl.ds(0, nk - 1)], small_send.at[R4])


def shards(mesh, tokens, grad_out, route_token, route_count, route_prob, w_gate, w_up, w_down):
    ng = mesh.shape["group"]
    ny = route_token.shape[2]
    cap = route_token.shape[3]
    nk = mesh.shape["member"] // ny
    hs, features = w_gate.shape[1:]
    cw = features // CLASSES
    assert cw % LANES == 0 and nk % (2 * CLASSES) == 0
    ns, tg, half, units = ng * cap, ny * nk, ng * cap // 2, cw // LANES
    low = -(-units // 8) * 8
    vmem = pl.BlockSpec(memory_space=pltpu.VMEM)
    hbm = pl.BlockSpec(memory_space=pl.ANY)
    dma = pltpu.SemaphoreType.DMA
    grad_shape = jax.ShapeDtypeStruct((1, hs, features), BF16)
    operands = (tokens, grad_out, route_token, route_count, route_prob, w_gate, w_up, w_down)
    return pl.pallas_call(
        functools.partial(kernel, (ng, ny, nk // 2, hs, cap, cw)),
        out_shape=(
            jax.ShapeDtypeStruct((1, features), BF16),
            grad_shape,
            grad_shape,
            grad_shape,
        ),
        in_specs=[hbm] * 8,
        out_specs=(vmem,) * 4,
        scratch_shapes=[
            pltpu.VMEM((1, features), BF16),
            pltpu.VMEM((1, features), BF16),
            pltpu.VMEM(route_token.shape, jnp.int32),
            pltpu.VMEM(route_count.shape, jnp.int32),
            pltpu.VMEM(route_prob.shape, F32),
            pltpu.VMEM((2 * CLASSES, low, LANES), F32),
            pltpu.VMEM((nk, low, LANES), F32),
            pltpu.VMEM((ny, nk, cw), BF16),
            pltpu.VMEM((ng, cap, cw), BF16),
            pltpu.VMEM((2, CLASSES, ns, cw), BF16),
            pltpu.VMEM((2 * hs, features), BF16),
            pltpu.VMEM((2 * hs, features), BF16),
            pltpu.VMEM((2, 2 * hs, cw), BF16),
            pltpu.VMEM((ns, 2 * hs), F32),
            pltpu.VMEM((ns, 2 * hs), F32),
            pltpu.VMEM((2, ns, 2 * hs), BF16),
            pltpu.VMEM((2 * hs, ns), BF16),
            pltpu.VMEM((hs, ns), BF16),
            pltpu.VMEM((2, half, cw), F32),
            pltpu.VMEM((2, half, cw), BF16),
            pltpu.VMEM((2, half, cw), BF16),
            pltpu.VMEM((ng, cap, cw), BF16),
            pltpu.VMEM((ng, cap, cw), BF16),
            pltpu.VMEM((ny, nk, cw), BF16),
            pltpu.VMEM((ny, nk, cw), BF16),
            pltpu.VMEM((nk, low, LANES), F32),
            pltpu.VMEM((nk, low, LANES), F32),
            dma((5,)),
            dma((4,)),
            dma((8,)),
            dma((8,)),
            dma((4,)),
            dma((4,)),
            dma((5,)),
            dma((5,)),
            dma((2,)),
            dma((2,)),
        ],
        compiler_params=pltpu.CompilerParams(
            collective_id=0, has_side_effects=True, vmem_limit_bytes=32 * 1024 * 1024
        ),
        name="routed_backward",
    )(*[pltpu.with_memory_space_constraint(a, pltpu.HBM) for a in operands])


def solution(mesh):
    both = ("group", "member")
    return jax.shard_map(
        functools.partial(shards, mesh),
        mesh=mesh,
        in_specs=(
            P(both, None),
            P(both, None),
            P("group", None, None, None),
            P("group", None, None),
            P("group", None, None, None),
            P(both, None, None),
            P(both, None, None),
            P(both, None, None),
        ),
        out_specs=(
            P(both, None),
            P(both, None, None),
            P(both, None, None),
            P(both, None, None),
        ),
        check_vma=False,
    )
```

time: 725 us -> 83.5 us (0.12)
  blocking collectives: 618 us -> 0 us
  Pallas kernels: 0 us -> 79.8 us
  waiting for transfers between devices: 64.2 us -> 0 us
  starting transfers between devices: 19.7 us -> 0 us
  matrix products: 8.98 us -> 0 us
    unnamed x1 -> x0, blocking collectives: 506 us -> none
    all_gather x2 -> x0, blocking collectives: 112 us -> none  [the longest x1 62.5 us: shards(): lax.all_gather(tokens, 'member', axis=0, tiled=True)]
    pallas_call x0 -> x1, Pallas kernels: none -> 79.8 us  [shards(): pl.pallas_call(functools.partial(kernel, (ng, ny, nk // 2, hs, cap, cw)),...]
    all_to_all x3 -> x0, waiting for transfers between devices: 64.2 us -> none  [the longest x1 38.7 us: shards(): lax.all_to_all(partial_rows.reshape(groups, capacity, features), 'group',...]
    all_to_all x3 -> x0, starting transfers between devices: 19.7 us -> none  [the longest x1 8.35 us: shards(): lax.all_to_all(send_x, 'group', split_axis=0, concat_axis=0, tiled=True)]
    dot_general x9 -> x0, matrix products: 8.98 us -> none  [the longest x1 2.53 us: shards(): jnp.dot(selector, returned, precision=lax.Precision.HIGHEST, preferred_el...]
  transfers between devices with their start and end apart: 3 -> 0, of which waited for: 2 -> 0; matrix products, arithmetic and copies ran while one was open for 1% -> 0% of each run, Pallas kernels for 0% -> 0%
where the time goes in v2:
time: 83.5 us; the launch traced here: 83.4 us
  Pallas kernels  79.8 us (96%)
  local copies, waits for them, and re-layouts  2.9 us (3%)
    pallas_call x1, Pallas kernels, shards(): pl.pallas_call(functools.partial(kernel, (ng, ny, nk // 2, hs, cap, cw)),...  79.8 us
    unnamed x4, local copies, waits for them, and re-layouts  2.9 us

profile of v2, /device:TPU:1, one launch (start us, length us, event | category | flops | bytes accessed | tf_op | source)
XLA Modules:
  0.0 83.4 jit_solution(4036134821558199659)
XLA Ops:
  0.6 79.8 %routed_backward.1 = (bf16[1,3584]{1,0:T(2,128)(2,1)S(1)}, bf16[1,64,3584]{2,1,0:T(8,128)(2,1)S(1)}, bf16[1,64,3584]{2,1,0:T(8,128)(2,1)S(1)}, bf16[1,64,3584]{2,1,0:T(8,128)(2,1)S(1)}) custom-call(bf16[1,3584]{1,0:T(2,128)(2,1)} %x_hbm.1, bf16[1,3584]{1,0:T(2,128)(2,1)} %dy_hbm.1, s32[1,8,8,16]{3,2,1,0:T(8,128)} %tok_hbm.1, s32[1,8,8]{2,1,0:T(8,128)} %cnt_hbm.1, ...), custom_call_target="tpu_custom_call" | custom-call | tf_op jit(solution)/shard_map/routed_backward/pallas_call | solution.py:346
  80.4 0.6 copy.16
  81.1 0.8 copy.17
  81.8 0.8 copy.18
  82.6 0.8 copy.19

commit v3 on v2

--- a/solution.py
+++ b/solution.py
@@ -20,6 +20,10 @@
 
 def dot_nt(a, b):
     return lax.dot_general(a, b, (((1,), (1,)), ((), ())), preferred_element_type=F32)
+
+
+def far_first(n):
+    return sorted(range(1, n), key=lambda o: -min(o, n - o))
 
 
 def kernel(
@@ -40,7 +44,12 @@
     half = ns // 2
     span = ng // 2
     units = cw // LANES
-    pieces = [slice(o, min(o + 256, cw)) for o in range(0, cw, 256)]
+    cut = -(-units // 2) * LANES
+    parts = (pl.ds(0, cut), pl.ds(cut, cw - cut))
+    pieces = [
+        [slice(o, min(o + 256, hi)) for o in range(lo, hi, 256)]
+        for lo, hi in ((0, cut), (cut, cw))
+    ]
 
     z = lax.axis_index("group")
     m = lax.axis_index("member")
@@ -72,13 +81,13 @@
             pltpu.get_barrier_semaphore(), inc=1, device_id=device, device_id_type=MESH
         )
 
-    A, B, C, W, X, R2, R3, R4 = range(8)
-
-    for o in range(1, nk):
+    A, W, X, R4, B, C, R2, R3 = 0, 1, 2, 3, 4, 6, 8, 10
+
+    for o in far_first(nk):
         signal((z, y * nk + (k + o) % nk))
-    for o in range(1, ny):
+    for o in far_first(ny):
         signal((z, ((y + o) % ny) * nk + k))
-    for o in range(1, ng):
+    for o in far_first(ng):
         signal(((z + o) % ng, m))
 
     inputs = [
@@ -111,7 +120,7 @@
 
     pl.semaphore_wait(pltpu.get_barrier_semaphore(), (nk - 1) + (ny - 1) + (ng - 1))
 
-    for o in range(1, nk):
+    for o in far_first(nk):
         kk = (k + o) % nk
         remote(
             send_a.at[(kk % 2) * CLASSES + kk // 2 % CLASSES], recv_a.at[k], small_send.at[A], small_recv.at[A],
@@ -164,57 +173,78 @@
 
     arrived(recv_a.at[pl.ds(0, nk - 1)], small_recv.at[A])
     t_all[y] = jnp.concatenate([recv_a[:, u, :] for u in range(units)], axis=1).astype(BF16)
-    for o in range(1, ny):
+    for p, part in enumerate(parts):
+        if p:
+            arrived(t_all.at[pl.ds(0, ny - 1), :, parts[0]], small_send.at[B])
+        for o in far_first(ny):
+            block = t_all.at[y, :, part]
+            remote(
+                block, block, small_send.at[B + p], small_recv.at[B + p],
+                (z, ((y + o) % ny) * nk + k),
+            ).start()
+    here = pl.ds(pl.multiple_of(z * cap, cap), cap)
+    for p, part in enumerate(parts):
+        arrived(t_all.at[pl.ds(0, ny - 1), :, part], small_recv.at[B + p])
+        for piece in pieces[p]:
+            width = piece.stop - piece.start
+            picked = dot_nn(sel, t_all[:, :, piece].reshape(tg, width)) * factor
+            z_send[:, :, piece] = picked.astype(BF16).reshape(ng, cap, width)
+        if p:
+            arrived(z_send.at[pl.ds(0, ng - 1), :, parts[0]], small_send.at[C])
+        for o in far_first(ng):
+            g = (z + o) % ng
+            remote(
+                z_send.at[g, :, part], rows.at[c, brings, here, part],
+                small_send.at[C + p], small_recv.at[C + p], (g, m),
+            ).start()
+    rows[c, brings, here, :] = z_send[z]
+
+    moves = ((1, 0), (-1, 0), (1, 1), (-1, 1), (2, 0), (-2, 1))
+    goes_on = {0: 4, 3: 5}
+
+    def source(steps):
+        return (brings + CLASSES - steps) % CLASSES
+
+    def pass_on(quarter, i):
+        steps, p = moves[i]
+        block = rows.at[c, quarter, :, parts[p]]
         remote(
-            t_all.at[y], t_all.at[y], small_send.at[B], small_recv.at[B],
-            (z, ((y + o) % ny) * nk + k),
+            block, block, ring_send.at[i], ring_recv.at[i], along(1 if steps > 0 else -1)
         ).start()
-    arrived(t_all.at[pl.ds(0, ny - 1)], small_recv.at[B])
-    for piece in pieces:
-        width = piece.stop - piece.start
-        picked = dot_nn(sel, t_all[:, :, piece].reshape(tg, width)) * factor
-        z_send[:, :, piece] = picked.astype(BF16).reshape(ng, cap, width)
-    here = pl.ds(pl.multiple_of(z * cap, cap), cap)
-    for o in range(1, ng):
-        g = (z + o) % ng
-        remote(
-            z_send.at[g], rows.at[c, brings, here, :], small_send.at[C], small_recv.at[C],
-            (g, m),
-        ).start()
-    rows[c, brings, here, :] = z_send[z]
-    arrived(rows.at[c, brings, pl.ds(0, ns - cap), :], small_recv.at[C])
-
-    whole, first, second = pl.ds(0, ns), pl.ds(0, half), pl.ds(half, half)
-    moves = ((1, whole), (-1, whole), (2, first), (-2, second))
-    for i, (steps, part) in enumerate(moves):
-        block = rows.at[c, brings, part, :]
-        remote(block, block, ring_send.at[i], ring_recv.at[i], along(steps)).start()
-
-    def share(quarter, part, i):
-        block = rows.at[c, quarter, part, :]
-        return remote(block, block, sib_send.at[i], sib_recv.at[i], sibling)
+
+    def share(quarter, p, i):
+        block = rows.at[c, quarter, :, parts[p]]
+        remote(block, block, sib_send.at[i], sib_recv.at[i], sibling).start()
 
     def accumulate(quarter):
         cols = pl.ds(pl.multiple_of(quarter * cw, LANES), cw)
         acc_gu[...] += dot_nt(rows[0, quarter], w_gu[:, cols])
         acc_dh[...] += dot_nt(rows[1, quarter], w_dd[:, cols])
 
-    def source(steps):
-        return (brings + CLASSES - steps) % CLASSES
-
-    share(brings, whole, 4).start()
-    arrived(rows.at[1 - c, brings], sib_recv.at[4])
-    accumulate(brings)
-    for stage in (0, 2):
-        for i in (stage, stage + 1):
-            steps, part = moves[i]
-            arrived(rows.at[c, source(steps), part, :], ring_recv.at[i])
-            share(source(steps), part, i).start()
-        for i in (stage, stage + 1):
-            steps, part = moves[i]
-            arrived(rows.at[1 - c, source(steps), part, :], sib_recv.at[i])
-            if i != 2:
-                accumulate(source(steps))
+    for p, part in enumerate(parts):
+        arrived(rows.at[c, brings, pl.ds(0, ns - cap), part], small_recv.at[C + p])
+        if p:
+            for i in (0, 1):
+                arrived(rows.at[0, 0, :, parts[0]], ring_send.at[i])
+        pass_on(brings, 2 * p)
+        pass_on(brings, 2 * p + 1)
+        share(brings, p, 6 + p)
+    for i in range(6):
+        steps, p = moves[i]
+        arrived(rows.at[c, source(steps), :, parts[p]], ring_recv.at[i])
+        if i in goes_on:
+            pass_on(source(steps), goes_on[i])
+        share(source(steps), p, i)
+        if i == 1:
+            for p in range(2):
+                arrived(rows.at[1 - c, brings, :, parts[p]], sib_recv.at[6 + p])
+            accumulate(brings)
+        if i in (3, 5):
+            for j in (0, 1, 2, 3) if i == 3 else (4, 5):
+                steps, p = moves[j]
+                arrived(rows.at[1 - c, source(steps), :, parts[p]], sib_recv.at[j])
+                if j in (2, 3, 5):
+                    accumulate(source(steps))
 
     both = acc_gu[...]
     turned = pltpu.roll(both, hs, 1)
@@ -234,7 +264,7 @@
     h_t[...] = (active * up).T[0:hs, :].astype(BF16)
 
     def gradients(quarter):
-        for piece in pieces:
+        for piece in pieces[0] + pieces[1]:
             cols = slice(quarter * cw + piece.start, quarter * cw + piece.stop)
             pair = dot_nn(d_t[...], rows[0, quarter, :, piece]).astype(BF16)
             gg[0, :, cols] = pair[0:hs]
@@ -252,71 +282,86 @@
     arrived(w_sib, small_recv.at[W])
     arrived(d_pair.at[0], small_recv.at[X])
 
+    for p, part in enumerate(parts):
+        for h in range(2):
+            for piece in pieces[p]:
+                snd[h, :, piece] = partial(other, h, piece).astype(BF16)
+            if p:
+                arrived(snd.at[h, :, parts[0]], red_send.at[0, h])
+            remote(
+                snd.at[h, :, part], rcv.at[h, :, part], red_send.at[p, h], red_recv.at[p, h],
+                neighbour[h],
+            ).start()
     for h in range(2):
-        for piece in pieces:
-            snd[h, :, piece] = partial(other, h, piece).astype(BF16)
-        remote(snd.at[h], rcv.at[h], red_send.at[h], red_recv.at[h], neighbour[h]).start()
-    for h in range(2):
-        for piece in pieces:
+        for piece in pieces[0] + pieces[1]:
             p_buf[h, :, piece] = partial(own, h, piece)
     gradients(0)
+
+    for p, part in enumerate(parts):
+        for h in range(2):
+            arrived(rcv.at[h, :, part], red_recv.at[p, h])
+            for piece in pieces[p]:
+                value = p_buf[h, :, piece] + rcv[h, :, piece].astype(F32)
+                r2_send[pl.ds(h * span, span), :, piece] = value.astype(BF16).reshape(
+                    span, cap, piece.stop - piece.start
+                )
+        if p:
+            arrived(r2_send.at[pl.ds(0, ng - 1), :, parts[0]], small_send.at[R2])
+        for o in far_first(ng):
+            s = (z + o) % ng
+            remote(
+                r2_send.at[s, :, part], r2_recv.at[z, :, part], small_send.at[R2 + p],
+                small_recv.at[R2 + p], (s, m),
+            ).start()
+    r2_recv[z] = r2_send[z]
     gradients(1)
-
+    gradients(2)
+    for p, part in enumerate(parts):
+        arrived(r2_recv.at[pl.ds(0, ng - 1), :, part], small_recv.at[R2 + p])
+        for piece in pieces[p]:
+            width = piece.stop - piece.start
+            summed = dot_nn(sel_t, r2_recv[:, :, piece].reshape(ns, width))
+            r3_send[:, :, piece] = summed.astype(BF16).reshape(ny, nk, width)
+        if p:
+            arrived(r3_send.at[pl.ds(0, ny - 1), :, parts[0]], small_send.at[R3])
+        for o in far_first(ny):
+            to = (y + o) % ny
+            remote(
+                r3_send.at[to, :, part], r3_recv.at[y, :, part], small_send.at[R3 + p],
+                small_recv.at[R3 + p], (z, to * nk + k),
+            ).start()
+    r3_recv[y] = r3_send[y]
+    gradients(3)
+    r4_send[...] = jnp.zeros_like(r4_send)
+
+    arrived(recv_a.at[pl.ds(0, nk - 1)], small_send.at[A])
+    arrived(t_all.at[pl.ds(0, ny - 1), :, parts[1]], small_send.at[B + 1])
+    arrived(z_send.at[pl.ds(0, ng - 1), :, parts[1]], small_send.at[C + 1])
+    arrived(w_sib, small_send.at[W])
+    for i, (steps, p) in enumerate(moves):
+        if i > 1:
+            arrived(rows.at[0, 0, :, parts[p]], ring_send.at[i])
+        arrived(rows.at[0, 0, :, parts[p]], sib_send.at[i])
+    for p, part in enumerate(parts):
+        arrived(rows.at[0, 0, :, part], sib_send.at[6 + p])
     for h in range(2):
-        arrived(rcv.at[h], red_recv.at[h])
-        value = p_buf[h] + rcv[h].astype(F32)
-        r2_send[pl.ds(h * span, span)] = value.astype(BF16).reshape(span, cap, cw)
-        for o in range(span):
-            s = h * span + (z + o) % span
-
-            @pl.when(s != z)
-            def _():
-                remote(
-                    r2_send.at[s], r2_recv.at[z], small_send.at[R2], small_recv.at[R2], (s, m)
-                ).start()
-
-    r2_recv[z] = r2_send[z]
-    gradients(2)
-    gradients(3)
-    arrived(r2_recv.at[pl.ds(0, ng - 1)], small_recv.at[R2])
-    for piece in pieces:
-        width = piece.stop - piece.start
-        summed = dot_nn(sel_t, r2_recv[:, :, piece].reshape(ns, width))
-        r3_send[:, :, piece] = summed.astype(BF16).reshape(ny, nk, width)
-    for o in range(1, ny):
-        to = (y + o) % ny
-        remote(
-            r3_send.at[to], r3_recv.at[y], small_send.at[R3], small_recv.at[R3],
-            (z, to * nk + k),
-        ).start()
-    r3_recv[y] = r3_send[y]
-    r4_send[...] = jnp.zeros_like(r4_send)
-
-    arrived(recv_a.at[pl.ds(0, nk - 1)], small_send.at[A])
-    arrived(t_all.at[pl.ds(0, ny - 1)], small_send.at[B])
-    arrived(z_send.at[pl.ds(0, ng - 1)], small_send.at[C])
-    arrived(w_sib, small_send.at[W])
-    for i, (steps, part) in enumerate(moves):
-        arrived(rows.at[0, 0, part, :], ring_send.at[i])
-        arrived(rows.at[0, 0, part, :], sib_send.at[i])
-    arrived(rows.at[0, 0], sib_send.at[4])
-    for h in range(2):
-        arrived(snd.at[h], red_send.at[h])
+        arrived(snd.at[h, :, parts[1]], red_send.at[1, h])
     exchange.wait_send()
-    arrived(r2_send.at[pl.ds(0, ng - 1)], small_send.at[R2])
-
-    arrived(r3_recv.at[pl.ds(0, ny - 1)], small_recv.at[R3])
-    for u in range(units):
-        cols = slice(u * LANES, (u + 1) * LANES)
-        r4_send[:, u, :] = jnp.sum(r3_recv[:, :, cols].astype(F32), axis=0)
-    for o in range(1, nk):
+    arrived(r2_send.at[pl.ds(0, ng - 1), :, parts[1]], small_send.at[R2 + 1])
+
+    for p, part in enumerate(parts):
+        arrived(r3_recv.at[pl.ds(0, ny - 1), :, part], small_recv.at[R3 + p])
+        for u in range(p * cut // LANES, units if p else cut // LANES):
+            cols = slice(u * LANES, (u + 1) * LANES)
+            r4_send[:, u, :] = jnp.sum(r3_recv[:, :, cols].astype(F32), axis=0)
+    for o in far_first(nk):
         to = (k + o) % nk
         remote(
             r4_send.at[to], r4_recv.at[k], small_send.at[R4], small_recv.at[R4],
             (z, y * nk + to),
         ).start()
     r4_recv[k] = r4_send[k]
-    arrived(r3_send.at[pl.ds(0, ny - 1)], small_send.at[R3])
+    arrived(r3_send.at[pl.ds(0, ny - 1), :, parts[1]], small_send.at[R3 + 1])
     arrived(r4_recv.at[pl.ds(0, nk - 1)], small_recv.at[R4])
     for quarter in range(CLASSES):
         total = r4_recv[quarter]
@@ -383,14 +428,14 @@
             pltpu.VMEM((nk, low, LANES), F32),
             dma((5,)),
             dma((4,)),
+            dma((12,)),
+            dma((12,)),
+            dma((6,)),
+            dma((6,)),
             dma((8,)),
             dma((8,)),
-            dma((4,)),
-            dma((4,)),
-            dma((5,)),
-            dma((5,)),
-            dma((2,)),
-            dma((2,)),
+            dma((2, 2)),
+            dma((2, 2)),
         ],
         compiler_params=pltpu.CompilerParams(
             collective_id=0, has_side_effects=True, vmem_limit_bytes=32 * 1024 * 1024

time: 83.5 us -> 79.9 us (0.957)
  Pallas kernels: 79.8 us -> 76.1 us
    pallas_call x1, Pallas kernels: 79.8 us -> 76.1 us  [shards(): pl.pallas_call(functools.partial(kernel, (ng, ny, nk // 2, hs, cap, cw)),...]
where the time goes in v3:
time: 79.9 us; the launch traced here: 79.7 us
  Pallas kernels  76.1 us (95%)
  local copies, waits for them, and re-layouts  2.9 us (4%)
    pallas_call x1, Pallas kernels, shards(): pl.pallas_call(functools.partial(kernel, (ng, ny, nk // 2, hs, cap, cw)),...  76.1 us
    unnamed x4, local copies, waits for them, and re-layouts  2.9 us

profile of v3, /device:TPU:1, one launch (start us, length us, event | category | flops | bytes accessed | tf_op | source)
XLA Modules:
  0.0 79.7 jit_solution(309851047789319191)
XLA Ops:
  0.6 76.1 %routed_backward.1 = (bf16[1,3584]{1,0:T(2,128)(2,1)S(1)}, bf16[1,64,3584]{2,1,0:T(8,128)(2,1)S(1)}, bf16[1,64,3584]{2,1,0:T(8,128)(2,1)S(1)}, bf16[1,64,3584]{2,1,0:T(8,128)(2,1)S(1)}) custom-call(bf16[1,3584]{1,0:T(2,128)(2,1)} %x_hbm.1, bf16[1,3584]{1,0:T(2,128)(2,1)} %dy_hbm.1, s32[1,8,8,16]{3,2,1,0:T(8,128)} %tok_hbm.1, s32[1,8,8]{2,1,0:T(8,128)} %cnt_hbm.1, ...), custom_call_target="tpu_custom_call" | custom-call | tf_op jit(solution)/shard_map/routed_backward/pallas_call | solution.py:391
  76.8 0.6 copy.16
  77.4 0.8 copy.17
  78.1 0.8 copy.18
  78.9 0.8 copy.19

commit v4 on v3

--- a/solution.py
+++ b/solution.py
@@ -223,9 +223,6 @@
 
     for p, part in enumerate(parts):
         arrived(rows.at[c, brings, pl.ds(0, ns - cap), part], small_recv.at[C + p])
-        if p:
-            for i in (0, 1):
-                arrived(rows.at[0, 0, :, parts[0]], ring_send.at[i])
         pass_on(brings, 2 * p)
         pass_on(brings, 2 * p + 1)
         share(brings, p, 6 + p)
@@ -286,8 +283,6 @@
         for h in range(2):
             for piece in pieces[p]:
                 snd[h, :, piece] = partial(other, h, piece).astype(BF16)
-            if p:
-                arrived(snd.at[h, :, parts[0]], red_send.at[0, h])
             remote(
                 snd.at[h, :, part], rcv.at[h, :, part], red_send.at[p, h], red_recv.at[p, h],
                 neighbour[h],
@@ -305,8 +300,6 @@
                 r2_send[pl.ds(h * span, span), :, piece] = value.astype(BF16).reshape(
                     span, cap, piece.stop - piece.start
                 )
-        if p:
-            arrived(r2_send.at[pl.ds(0, ng - 1), :, parts[0]], small_send.at[R2])
         for o in far_first(ng):
             s = (z + o) % ng
             remote(
@@ -322,8 +315,6 @@
             width = piece.stop - piece.start
             summed = dot_nn(sel_t, r2_recv[:, :, piece].reshape(ns, width))
             r3_send[:, :, piece] = summed.astype(BF16).reshape(ny, nk, width)
-        if p:
-            arrived(r3_send.at[pl.ds(0, ny - 1), :, parts[0]], small_send.at[R3])
         for o in far_first(ny):
             to = (y + o) % ny
             remote(
@@ -339,15 +330,16 @@
     arrived(z_send.at[pl.ds(0, ng - 1), :, parts[1]], small_send.at[C + 1])
     arrived(w_sib, small_send.at[W])
     for i, (steps, p) in enumerate(moves):
-        if i > 1:
-            arrived(rows.at[0, 0, :, parts[p]], ring_send.at[i])
+        arrived(rows.at[0, 0, :, parts[p]], ring_send.at[i])
         arrived(rows.at[0, 0, :, parts[p]], sib_send.at[i])
     for p, part in enumerate(parts):
         arrived(rows.at[0, 0, :, part], sib_send.at[6 + p])
     for h in range(2):
-        arrived(snd.at[h, :, parts[1]], red_send.at[1, h])
+        for p, part in enumerate(parts):
+            arrived(snd.at[h, :, part], red_send.at[p, h])
     exchange.wait_send()
-    arrived(r2_send.at[pl.ds(0, ng - 1), :, parts[1]], small_send.at[R2 + 1])
+    for p, part in enumerate(parts):
+        arrived(r2_send.at[pl.ds(0, ng - 1), :, part], small_send.at[R2 + p])
 
     for p, part in enumerate(parts):
         arrived(r3_recv.at[pl.ds(0, ny - 1), :, part], small_recv.at[R3 + p])
@@ -361,7 +353,8 @@
             (z, y * nk + to),
         ).start()
     r4_recv[k] = r4_send[k]
-    arrived(r3_send.at[pl.ds(0, ny - 1), :, parts[1]], small_send.at[R3 + 1])
+    for p, part in enumerate(parts):
+        arrived(r3_send.at[pl.ds(0, ny - 1), :, part], small_send.at[R3 + p])
     arrived(r4_recv.at[pl.ds(0, nk - 1)], small_recv.at[R4])
     for quarter in range(CLASSES):
         total = r4_recv[quarter]

time: 79.9 us -> 77.9 us (0.975)
  Pallas kernels: 76.1 us -> 74.2 us
    pallas_call x1, Pallas kernels: 76.1 us -> 74.2 us  [shards(): pl.pallas_call(functools.partial(kernel, (ng, ny, nk // 2, hs, cap, cw)),...]
where the time goes in v4:
time: 77.9 us; the launch traced here: 77.7 us
  Pallas kernels  74.2 us (95%)
  local copies, waits for them, and re-layouts  2.9 us (4%)
    pallas_call x1, Pallas kernels, shards(): pl.pallas_call(functools.partial(kernel, (ng, ny, nk // 2, hs, cap, cw)),...  74.2 us
    unnamed x4, local copies, waits for them, and re-layouts  2.9 us

profile of v4, /device:TPU:1, one launch (start us, length us, event | category | flops | bytes accessed | tf_op | source)
XLA Modules:
  0.0 77.7 jit_solution(7935032500573184890)
XLA Ops:
  0.6 74.2 %routed_backward.1 = (bf16[1,3584]{1,0:T(2,128)(2,1)S(1)}, bf16[1,64,3584]{2,1,0:T(8,128)(2,1)S(1)}, bf16[1,64,3584]{2,1,0:T(8,128)(2,1)S(1)}, bf16[1,64,3584]{2,1,0:T(8,128)(2,1)S(1)}) custom-call(bf16[1,3584]{1,0:T(2,128)(2,1)} %x_hbm.1, bf16[1,3584]{1,0:T(2,128)(2,1)} %dy_hbm.1, s32[1,8,8,16]{3,2,1,0:T(8,128)} %tok_hbm.1, s32[1,8,8]{2,1,0:T(8,128)} %cnt_hbm.1, ...), custom_call_target="tpu_custom_call" | custom-call | tf_op jit(solution)/shard_map/routed_backward/pallas_call | solution.py:384
  74.8 0.6 copy.16
  75.4 0.8 copy.17
  76.2 0.8 copy.18
  77.0 0.8 copy.19

commit v5 on v4

--- a/solution.py
+++ b/solution.py
@@ -44,7 +44,7 @@
     half = ns // 2
     span = ng // 2
     units = cw // LANES
-    cut = -(-units // 2) * LANES
+    cut = max(units // 2, 1) * LANES
     parts = (pl.ds(0, cut), pl.ds(cut, cw - cut))
     pieces = [
         [slice(o, min(o + 256, hi)) for o in range(lo, hi, 256)]
@@ -174,8 +174,6 @@
     arrived(recv_a.at[pl.ds(0, nk - 1)], small_recv.at[A])
     t_all[y] = jnp.concatenate([recv_a[:, u, :] for u in range(units)], axis=1).astype(BF16)
     for p, part in enumerate(parts):
-        if p:
-            arrived(t_all.at[pl.ds(0, ny - 1), :, parts[0]], small_send.at[B])
         for o in far_first(ny):
             block = t_all.at[y, :, part]
             remote(
@@ -189,8 +187,6 @@
             width = piece.stop - piece.start
             picked = dot_nn(sel, t_all[:, :, piece].reshape(tg, width)) * factor
             z_send[:, :, piece] = picked.astype(BF16).reshape(ng, cap, width)
-        if p:
-            arrived(z_send.at[pl.ds(0, ng - 1), :, parts[0]], small_send.at[C])
         for o in far_first(ng):
             g = (z + o) % ng
             remote(
@@ -326,8 +322,10 @@
     r4_send[...] = jnp.zeros_like(r4_send)
 
     arrived(recv_a.at[pl.ds(0, nk - 1)], small_send.at[A])
-    arrived(t_all.at[pl.ds(0, ny - 1), :, parts[1]], small_send.at[B + 1])
-    arrived(z_send.at[pl.ds(0, ng - 1), :, parts[1]], small_send.at[C + 1])
+    for p, part in enumerate(parts):
+        arrived(t_all.at[pl.ds(0, ny - 1), :, part], small_send.at[B + p])
+    for p, part in enumerate(parts):
+        arrived(z_send.at[pl.ds(0, ng - 1), :, part], small_send.at[C + p])
     arrived(w_sib, small_send.at[W])
     for i, (steps, p) in enumerate(moves):
         arrived(rows.at[0, 0, :, parts[p]], ring_send.at[i])

time: 77.9 us -> 77.8 us (level)
  no operation moved by 1% of the time
where the time goes in v5:
time: 77.8 us; the launch traced here: 77.6 us
  Pallas kernels  74 us (95%)
  local copies, waits for them, and re-layouts  2.9 us (4%)
    pallas_call x1, Pallas kernels, shards(): pl.pallas_call(functools.partial(kernel, (ng, ny, nk // 2, hs, cap, cw)),...  74 us
    unnamed x4, local copies, waits for them, and re-layouts  2.9 us

profile of v5, /device:TPU:1, one launch (start us, length us, event | category | flops | bytes accessed | tf_op | source)
XLA Modules:
  0.0 77.6 jit_solution(6239559484491954322)
XLA Ops:
  0.6 74.0 %routed_backward.1 = (bf16[1,3584]{1,0:T(2,128)(2,1)S(1)}, bf16[1,64,3584]{2,1,0:T(8,128)(2,1)S(1)}, bf16[1,64,3584]{2,1,0:T(8,128)(2,1)S(1)}, bf16[1,64,3584]{2,1,0:T(8,128)(2,1)S(1)}) custom-call(bf16[1,3584]{1,0:T(2,128)(2,1)} %x_hbm.1, bf16[1,3584]{1,0:T(2,128)(2,1)} %dy_hbm.1, s32[1,8,8,16]{3,2,1,0:T(8,128)} %tok_hbm.1, s32[1,8,8]{2,1,0:T(8,128)} %cnt_hbm.1, ...), custom_call_target="tpu_custom_call" | custom-call | tf_op jit(solution)/shard_map/routed_backward/pallas_call | solution.py:382
  74.7 0.6 copy.16
  75.3 0.8 copy.17
  76.0 0.8 copy.18
  76.8 0.8 copy.19
